TPU v7x, 256 devices: a whole 4x4x8 slice. The times are simulated.
256 devices in a mesh: dom: 32 (over y, z_lo, x), rep: 8 (over z_hi, core).
Axes of the slice: x: 4, y: 4, z: 8 (z_hi: 4, z_lo: 2; z = z_hi * 2 + z_lo), core: 2. Of those that a mesh axis runs over, the one named last changes fastest.
Arguments:
- codes: bfloat16 [65536, 256], P('dom'), may hold values from -1.5 to 1.5
- scales: bfloat16 [65536], P('dom'), may hold values from 0.5 to 2
- accum: float32 [65536], P('dom'), may hold values from 0.01 to 1
- relations: bfloat16 [64, 256], replicated, may hold values from -5 to 5
- matching: int32 [32], P('dom'), may hold values from 0 to 31, as said below
- edges: int32 [3, 1048576], P(None, ('dom', 'rep')), may hold values from 0 to 2047, as said below
- counts: int32 [256], P(('dom', 'rep')), may hold values from 1 to 4096, 524288 in all
- negatives: int32 [2048, 1024], P(('dom', 'rep')), may hold values from 0 to 2047
Outputs:
- new_codes: bfloat16 [65536, 256], P('dom')
- new_accum: float32 [65536], P(('dom', 'rep'))
Inputs may be any that keep to these rules, and one draw needn't show every extreme that they name: matching[b] = b XOR m for one m from 1 to 31 shared by all buckets, so partitions pair up. `edges`: rows 0 and 2 hold row ids below 2048, row 1 relation ids below 64.
All inputs are finite; a program needn't handle non-finite values. No bound on the sum of `counts` on one device may be relied on, other than what follows from the above.
Results may differ from a plain program's by a relative error of at most 0.0075.
Values may be sent and summed in bfloat16 or wider, within the bound.
A program may use at most 64 MiB of HBM per device.

v0:
```python
import jax
import jax.numpy as jnp
from jax import lax
from jax.sharding import PartitionSpec as P

GROUP = 512


LEARN_RATE = 0.1
ROOT_EPSILON = 1e-08


def from_partner(block, axis, apart):
    count = lax.axis_size(axis)
    route = []
    for low in range(count):
        high = low | 1 << apart
        if high != low and high < count:
            route += [(low, high), (high, low)]
    return lax.ppermute(block, axis, route)


def group_terms(src_block, dst_block, relation_rows, src_ids, dst_ids, live_mask, negative_ids):
    source_rows = jnp.take(src_block, src_ids, axis=0).astype(jnp.float32)
    target_rows = jnp.take(dst_block, dst_ids, axis=0)
    negative_rows = jnp.take(dst_block, negative_ids, axis=0)
    query = (source_rows * relation_rows).astype(jnp.bfloat16)
    positive = jnp.sum(query.astype(jnp.float32) * target_rows.astype(jnp.float32), axis=1)
    scores = jnp.dot(query, negative_rows.T, preferred_element_type=jnp.float32)
    weight = live_mask.astype(jnp.float32)
    pos_coef = -weight * jax.nn.sigmoid(-positive)
    neg_coef = (weight[:, None] * jax.nn.sigmoid(scores) / negative_rows.shape[0]).astype(
        jnp.bfloat16
    )
    query_grad = pos_coef[:, None] * target_rows.astype(jnp.float32) + jnp.dot(
        neg_coef, negative_rows, preferred_element_type=jnp.float32
    )
    source_grad = query_grad * relation_rows
    target_grad = pos_coef[:, None] * query.astype(jnp.float32)
    negative_grad = lax.dot_general(
        neg_coef, query, (((0,), (0,)), ((), ())), preferred_element_type=jnp.float32
    )
    return (source_grad, target_grad, negative_grad)


def partner_bit(partner_bits, bit_index):
    return jnp.bitwise_and(jnp.right_shift(partner_bits, bit_index), 1) == 1


def body(codes, scales, accum, relations, matching, edges, counts, negatives):
    dom_bits = lax.axis_size("dom").bit_length() - 1
    rep_count = lax.axis_size("rep")
    partner_bits = jnp.bitwise_xor(matching[0], lax.axis_index("dom"))
    values = codes.astype(jnp.float32) * scales.astype(jnp.float32)[:, None]
    src_block = values.astype(jnp.bfloat16)
    dst_block = src_block
    for bit_index in range(dom_bits):
        arrived = from_partner(dst_block, "dom", bit_index)
        dst_block = jnp.where(partner_bit(partner_bits, bit_index), arrived, dst_block)
    part_rows = codes.shape[0]
    slots = edges.shape[1]
    group_len = GROUP
    group_total = slots // group_len
    live_mask = (jnp.arange(slots, dtype=jnp.int32) < counts[0]).astype(jnp.int32)
    edge_pack = jnp.concatenate([edges, live_mask[None, :]], axis=0).reshape(
        4, group_total, group_len
    )
    rel_count = relations.shape[0]

    def group_step(position, carry):
        block_ids = lax.dynamic_index_in_dim(edge_pack, position, 1, keepdims=False)
        block_negs = lax.dynamic_index_in_dim(negatives, position, 0, keepdims=False)

        def score_group(grads_in):
            one_hot = jax.nn.one_hot(block_ids[1], rel_count, dtype=jnp.bfloat16)
            relation_rows = jnp.dot(one_hot, relations, preferred_element_type=jnp.float32)
            source_grad, target_grad, negative_grad = group_terms(
                src_block,
                dst_block,
                relation_rows,
                block_ids[0],
                block_ids[2],
                block_ids[3],
                block_negs,
            )
            first = grads_in[0].at[block_ids[0]].add(source_grad)
            second = grads_in[1].at[block_ids[2]].add(target_grad).at[block_negs].add(negative_grad)
            return (first, second)

        return lax.cond(jnp.any(block_ids[3] > 0), score_group, lambda grads_in: grads_in, carry)

    empty = jnp.zeros((part_rows, values.shape[1]), jnp.float32)
    src_grad, dst_grad = lax.fori_loop(0, group_total, group_step, (empty, empty))
    share_rows = part_rows // rep_count
    first_row = lax.axis_index("rep") * share_rows
    returned = dst_grad
    for bit_index in range(dom_bits):
        arrived = from_partner(returned.astype(jnp.bfloat16), "dom", bit_index).astype(
            returned.dtype
        )
        returned = jnp.where(partner_bit(partner_bits, bit_index), arrived, returned)
    summed = lax.psum(src_grad + returned, "rep")
    state = accum + jnp.mean(summed * summed, axis=1)
    updated = values - LEARN_RATE * summed / (jnp.sqrt(state)[:, None] + ROOT_EPSILON)
    new_codes = (updated / scales.astype(jnp.float32)[:, None]).astype(jnp.bfloat16)
    new_accum = lax.dynamic_slice_in_dim(state, first_row, share_rows, 0)
    return (new_codes, new_accum)


def solution(mesh):
    placed = (
        P("dom", None),
        P("dom"),
        P("dom"),
        P(),
        P("dom"),
        P(None, ("dom", "rep")),
        P(("dom", "rep")),
        P(("dom", "rep"), None),
    )
    return jax.shard_map(
        body,
        mesh=mesh,
        in_specs=placed,
        out_specs=(P("dom", None), P(("dom", "rep"))),
        check_vma=False,
    )
```

profile of v0, /device:TPU:1, one launch (start us, length us, event | category | flops | bytes accessed | tf_op | source)
XLA Modules:
  0.0 715.8 jit_solution(17450824745099724348)
XLA Ops:
  9.6 2.1 collective-permute-start
  12.4 20.9 %collective-permute-done = bf16[2048,256]{1,0:T(8,128)(2,1)} collective-permute-done((bf16[2048,256]{1,0:T(8,128)(2,1)S(1)}, bf16[2048,256]{1,0:T(8,128)(2,1)}, u32[]{:S(2)}, u32[]{:S(2)}) %collective-permute-start) | collective-permute-done | bytes 1048608 | tf_op jit(solution)/shard_map/ppermute | solution.py:20
  33.9 4.2 collective-permute-start.1
  38.1 21.8 %collective-permute-done.1 = bf16[2048,256]{1,0:T(8,128)(2,1)} collective-permute-done((bf16[2048,256]{1,0:T(8,128)(2,1)S(1)}, bf16[2048,256]{1,0:T(8,128)(2,1)}, u32[]{:S(2)}, u32[]{:S(2)}) %collective-permute-start.1) | collective-permute-done | bytes 1048608 | tf_op jit(solution)/shard_map/ppermute | solution.py:20
  61.9 21.1 %collective-permute-done.2 = bf16[2048,256]{1,0:T(8,128)(2,1)} collective-permute-done((bf16[2048,256]{1,0:T(8,128)(2,1)S(1)}, bf16[2048,256]{1,0:T(8,128)(2,1)}, u32[]{:S(2)}, u32[]{:S(2)}) %collective-permute-start.2) | collective-permute-done | bytes 1048608 | tf_op jit(solution)/shard_map/ppermute | solution.py:20
  85.7 20.3 %collective-permute-done.3 = bf16[2048,256]{1,0:T(8,128)(2,1)S(1)} collective-permute-done((bf16[2048,256]{1,0:T(8,128)(2,1)S(1)}, bf16[2048,256]{1,0:T(8,128)(2,1)S(1)}, u32[]{:S(2)}, u32[]{:S(2)}) %collective-permute-start.3) | collective-permute-done | bytes 1048608 | tf_op jit(solution)/shard_map/ppermute | solution.py:20
  106.1 2.8 collective-permute-start.4
  109.7 21.8 %collective-permute-done.4 = bf16[2048,256]{1,0:T(8,128)(2,1)S(1)} collective-permute-done((bf16[2048,256]{1,0:T(8,128)(2,1)S(1)}, bf16[2048,256]{1,0:T(8,128)(2,1)S(1)}, u32[]{:S(2)}, u32[]{:S(2)}) %collective-permute-start.4) | collective-permute-done | bytes 1048608 | tf_op jit(solution)/shard_map/ppermute | solution.py:20
  133.2 191.3 %while.15 = (s32[]{:T(128)}, f32[2048,256]{1,0:T(8,128)}, f32[2048,256]{1,0:T(8,128)S(1)}, s32[4,8,512]{2,1,0:T(8,128)S(1)}, bf16[2048,256]{1,0:T(8,128)(2,1)}, ...) while((s32[]{:T(128)}, f32[2048,256]{1,0:T(8,128)}, ...), condition=%wide.region_8.10_spmd, body=%wide.region_0.9_spmd.sunk | while | flops 828435456 | bytes 30310256 | solution.py:93
  134.7 45.3 %conditional.2 = ((f32[2048,256]{1,0:T(8,128)}, f32[2048,256]{1,0:T(8,128)S(1)})) conditional(s32[]{:T(128)} %convert_element_type.171, (f32[2048,256]{1,0:T(8,128)}, f32[2048,256]{1,0:T(8,128)S(1)}) %tuple.54, (s32[4,1,512]{2,1,0:T(1,128)S(1)}, bf16[2048,256]{1,0:T(8,128)(2,1)}, bf16[64,256]{1,0:T(8,128)(2,1)S(1)}, bf16[2048,256]{1,0:T(8,128)(2,1)S(1)}, ...), branch_computations={%region_2.2_spmd, %region_3.8_spmd} | conditional | flops 828434432 | bytes 30291596 | solution.py:90
  137.6 2.9 gather_fusion.1
  141.4 2.2 fusion.1
  144.3 5.0 gather_fusion
  156.0 6.4 scatter_fusion
  165.3 4.6 scatter_fusion.1
  169.9 2.7 fusion.12
  172.6 7.3 %scatter_fusion.2 = f32[2048,256]{1,0:T(8,128)S(1)} fusion(f32[2048,256]{1,0:T(8,128)S(1)} %scatter_fusion.1, s32[1024]{0:T(1024)S(1)} %bitcast.28, f32[1024,256]{1,0:T(8,128)} %fusion.12), kind=kCustom, calls=%fused_computation.5 | custom fusion | flops 262144 | bytes 3149824 | tf_op jit(solution)/shard_map/while/body/eval_jaxpr/cond/branch_1_fun/scatter-add | solution.py:87
  181.2 45.3 %conditional.2 = ((f32[2048,256]{1,0:T(8,128)}, f32[2048,256]{1,0:T(8,128)S(1)})) conditional(s32[]{:T(128)} %convert_element_type.171, (f32[2048,256]{1,0:T(8,128)}, f32[2048,256]{1,0:T(8,128)S(1)}) %tuple.54, (s32[4,1,512]{2,1,0:T(1,128)S(1)}, bf16[2048,256]{1,0:T(8,128)(2,1)}, bf16[64,256]{1,0:T(8,128)(2,1)S(1)}, bf16[2048,256]{1,0:T(8,128)(2,1)S(1)}, ...), branch_computations={%region_2.2_spmd, %region_3.8_spmd} | conditional | flops 828434432 | bytes 30291596 | solution.py:90
  184.1 2.9 gather_fusion.1
  187.9 2.2 fusion.1
  190.8 5.0 gather_fusion
  202.5 6.4 scatter_fusion
  211.8 4.6 scatter_fusion.1
  216.4 2.7 fusion.12
  219.1 7.3 %scatter_fusion.2 = f32[2048,256]{1,0:T(8,128)S(1)} fusion(f32[2048,256]{1,0:T(8,128)S(1)} %scatter_fusion.1, s32[1024]{0:T(1024)S(1)} %bitcast.28, f32[1024,256]{1,0:T(8,128)} %fusion.12), kind=kCustom, calls=%fused_computation.5 | custom fusion | flops 262144 | bytes 3149824 | tf_op jit(solution)/shard_map/while/body/eval_jaxpr/cond/branch_1_fun/scatter-add | solution.py:87
  227.7 45.3 %conditional.2 = ((f32[2048,256]{1,0:T(8,128)}, f32[2048,256]{1,0:T(8,128)S(1)})) conditional(s32[]{:T(128)} %convert_element_type.171, (f32[2048,256]{1,0:T(8,128)}, f32[2048,256]{1,0:T(8,128)S(1)}) %tuple.54, (s32[4,1,512]{2,1,0:T(1,128)S(1)}, bf16[2048,256]{1,0:T(8,128)(2,1)}, bf16[64,256]{1,0:T(8,128)(2,1)S(1)}, bf16[2048,256]{1,0:T(8,128)(2,1)S(1)}, ...), branch_computations={%region_2.2_spmd, %region_3.8_spmd} | conditional | flops 828434432 | bytes 30291596 | solution.py:90
  230.6 2.9 gather_fusion.1
  234.4 2.2 fusion.1
  237.4 5.0 gather_fusion
  249.1 6.4 scatter_fusion
  258.4 4.6 scatter_fusion.1
  262.9 2.7 fusion.12
  265.7 7.3 %scatter_fusion.2 = f32[2048,256]{1,0:T(8,128)S(1)} fusion(f32[2048,256]{1,0:T(8,128)S(1)} %scatter_fusion.1, s32[1024]{0:T(1024)S(1)} %bitcast.28, f32[1024,256]{1,0:T(8,128)} %fusion.12), kind=kCustom, calls=%fused_computation.5 | custom fusion | flops 262144 | bytes 3149824 | tf_op jit(solution)/shard_map/while/body/eval_jaxpr/cond/branch_1_fun/scatter-add | solution.py:87
  274.2 45.3 %conditional.2 = ((f32[2048,256]{1,0:T(8,128)}, f32[2048,256]{1,0:T(8,128)S(1)})) conditional(s32[]{:T(128)} %convert_element_type.171, (f32[2048,256]{1,0:T(8,128)}, f32[2048,256]{1,0:T(8,128)S(1)}) %tuple.54, (s32[4,1,512]{2,1,0:T(1,128)S(1)}, bf16[2048,256]{1,0:T(8,128)(2,1)}, bf16[64,256]{1,0:T(8,128)(2,1)S(1)}, bf16[2048,256]{1,0:T(8,128)(2,1)S(1)}, ...), branch_computations={%region_2.2_spmd, %region_3.8_spmd} | conditional | flops 828434432 | bytes 30291596 | solution.py:90
  277.1 2.9 gather_fusion.1
  280.9 2.2 fusion.1
  283.9 5.0 gather_fusion
  295.6 6.4 scatter_fusion
  304.9 4.6 scatter_fusion.1
  309.5 2.7 fusion.12
  312.2 7.3 %scatter_fusion.2 = f32[2048,256]{1,0:T(8,128)S(1)} fusion(f32[2048,256]{1,0:T(8,128)S(1)} %scatter_fusion.1, s32[1024]{0:T(1024)S(1)} %bitcast.28, f32[1024,256]{1,0:T(8,128)} %fusion.12), kind=kCustom, calls=%fused_computation.5 | custom fusion | flops 262144 | bytes 3149824 | tf_op jit(solution)/shard_map/while/body/eval_jaxpr/cond/branch_1_fun/scatter-add | solution.py:87
  325.0 21.3 %collective-permute-done.5 = bf16[2048,256]{1,0:T(8,128)(2,1)S(1)} collective-permute-done((bf16[2048,256]{1,0:T(8,128)(2,1)S(1)}, bf16[2048,256]{1,0:T(8,128)(2,1)S(1)}, u32[]{:S(2)}, u32[]{:S(2)}) %collective-permute-start.5) | collective-permute-done | bytes 1048608 | tf_op jit(solution)/shard_map/ppermute | solution.py:20
  346.6 183.6 %collective-permute-start.6 = (bf16[2048,256]{1,0:T(8,128)(2,1)S(1)}, bf16[2048,256]{1,0:T(8,128)(2,1)S(1)}, u32[]{:S(2)}, u32[]{:S(2)}) collective-permute-start(bf16[2048,256]{1,0:T(8,128)(2,1)S(1)} %fusion.7), channel_id=1, source_target_pairs={{0,16},{16,0},{8,24},{24,8},{32,48},{48,32},{40,56},{56,40},{64,80... | collective-permute-start | bytes 3145736 | tf_op jit(solution)/shard_map/ppermute | solution.py:20
  530.2 22.2 %collective-permute-done.6 = bf16[2048,256]{1,0:T(8,128)(2,1)S(1)} collective-permute-done((bf16[2048,256]{1,0:T(8,128)(2,1)S(1)}, bf16[2048,256]{1,0:T(8,128)(2,1)S(1)}, u32[]{:S(2)}, u32[]{:S(2)}) %collective-permute-start.6) | collective-permute-done | bytes 1048608 | tf_op jit(solution)/shard_map/ppermute | solution.py:20
  553.6 20.1 %collective-permute-done.7 = bf16[2048,256]{1,0:T(8,128)(2,1)S(1)} collective-permute-done((bf16[2048,256]{1,0:T(8,128)(2,1)S(1)}, bf16[2048,256]{1,0:T(8,128)(2,1)S(1)}, u32[]{:S(2)}, u32[]{:S(2)}) %collective-permute-start.7) | collective-permute-done | bytes 1048608 | tf_op jit(solution)/shard_map/ppermute | solution.py:20
  574.1 19.9 %collective-permute-done.8 = bf16[2048,256]{1,0:T(8,128)(2,1)S(1)} collective-permute-done((bf16[2048,256]{1,0:T(8,128)(2,1)S(1)}, bf16[2048,256]{1,0:T(8,128)(2,1)S(1)}, u32[]{:S(2)}, u32[]{:S(2)}) %collective-permute-start.8) | collective-permute-done | bytes 1048608 | tf_op jit(solution)/shard_map/ppermute | solution.py:20
  594.5 18.1 %collective-permute-done.9 = bf16[2048,256]{1,0:T(8,128)(2,1)S(1)} collective-permute-done((bf16[2048,256]{1,0:T(8,128)(2,1)S(1)}, bf16[2048,256]{1,0:T(8,128)(2,1)S(1)}, u32[]{:S(2)}, u32[]{:S(2)}) %collective-permute-start.9) | collective-permute-done | bytes 1048608 | tf_op jit(solution)/shard_map/ppermute | solution.py:20
  614.4 90.2 %all-reduce.2.cloned.1.call-done = f32[2048,256]{1,0:T(8,128)} async-done(((f32[2048,256]{1,0:T(8,128)}), f32[2048,256]{1,0:T(8,128)}) %all-reduce.2.cloned.1.call-update) | async-done | bytes 2097168 | tf_op jit(solution)/shard_map/psum | solution.py:102
  (174 shorter events, 79.9 us)
Async XLA Ops:
  7.2 26.1 %copy-start.6 = (bf16[2048,256]{1,0:T(8,128)(2,1)S(1)}, bf16[2048,256]{1,0:T(8,128)(2,1)}, u32[]{:S(2)}) copy-start(bf16[2048,256]{1,0:T(8,128)(2,1)} %param.14) | copy-start | bytes 3145732
  7.2 697.5 %all-reduce.2.cloned.1.call-start = ((), (), s32[]{:S(2)}) async-start(), calls=%async_computation | async-start | bytes 4194304 | tf_op jit(solution)/shard_map/psum | solution.py:102
  9.6 50.5 %copy-start.1 = (bf16[2048,256]{1,0:T(8,128)(2,1)}, bf16[2048,256]{1,0:T(8,128)(2,1)S(1)}, u32[]{:S(2)}) copy-start(bf16[2048,256]{1,0:T(8,128)(2,1)S(1)} %fusion.6) | copy-start | bytes 3145732
  9.6 23.7 %collective-permute-start = (bf16[2048,256]{1,0:T(8,128)(2,1)S(1)}, bf16[2048,256]{1,0:T(8,128)(2,1)}, u32[]{:S(2)}, u32[]{:S(2)}) collective-permute-start(bf16[2048,256]{1,0:T(8,128)(2,1)S(1)} %fusion.6), channel_id=1, source_target_pairs={{0,8},{8,0},{16,24},{24,16},{32,40},{40,32},{48,56},{56,48},{64,72... | collective-permute-start | bytes 3145736 | tf_op jit(solution)/shard_map/ppermute | solution.py:20
  33.9 26.0 %collective-permute-start.1 = (bf16[2048,256]{1,0:T(8,128)(2,1)S(1)}, bf16[2048,256]{1,0:T(8,128)(2,1)}, u32[]{:S(2)}, u32[]{:S(2)}) collective-permute-start(bf16[2048,256]{1,0:T(8,128)(2,1)S(1)} %broadcast_select_fusion.4), channel_id=1, source_target_pairs={{0,16},{16,0},{8,24},{24,8},{32,48},{48,32},{40,56},{56,40},{64,80... | collective-permute-start | bytes 3145736 | tf_op jit(solution)/shard_map/ppermute | solution.py:20
  60.0 23.0 %collective-permute-start.2 = (bf16[2048,256]{1,0:T(8,128)(2,1)S(1)}, bf16[2048,256]{1,0:T(8,128)(2,1)}, u32[]{:S(2)}, u32[]{:S(2)}) collective-permute-start(bf16[2048,256]{1,0:T(8,128)(2,1)S(1)} %broadcast_select_fusion.5), channel_id=1, source_target_pairs={{0,32},{32,0},{8,40},{40,8},{16,48},{48,16},{24,56},{56,24},{64,96... | collective-permute-start | bytes 3145736 | tf_op jit(solution)/shard_map/ppermute | solution.py:20
  84.4 25.2 %copy-start.10 = (s32[3,4096]{1,0:T(4,128)S(1)}, s32[3,4096]{1,0:T(4,128)}, u32[]{:S(2)}) copy-start(s32[3,4096]{1,0:T(4,128)} %param.19) | copy-start | bytes 147460
  84.4 21.6 %collective-permute-start.3 = (bf16[2048,256]{1,0:T(8,128)(2,1)S(1)}, bf16[2048,256]{1,0:T(8,128)(2,1)S(1)}, u32[]{:S(2)}, u32[]{:S(2)}) collective-permute-start(bf16[2048,256]{1,0:T(8,128)(2,1)S(1)} %broadcast_select_fusion.6), channel_id=1, source_target_pairs={{0,64},{64,0},{8,72},{72,8},{16,80},{80,16},{24,88},{88,24},{32,96... | collective-permute-start | bytes 3145736 | tf_op jit(solution)/shard_map/ppermute | solution.py:20
  106.1 25.4 %collective-permute-start.4 = (bf16[2048,256]{1,0:T(8,128)(2,1)S(1)}, bf16[2048,256]{1,0:T(8,128)(2,1)S(1)}, u32[]{:S(2)}, u32[]{:S(2)}) collective-permute-start(bf16[2048,256]{1,0:T(8,128)(2,1)S(1)} %broadcast_select_fusion.7), channel_id=1, source_target_pairs={{0,128},{128,0},{8,136},{136,8},{16,144},{144,16},{24,152},{152,24... | collective-permute-start | bytes 3145736 | tf_op jit(solution)/shard_map/ppermute | solution.py:20
  131.6 1.6 copy-start.9
  149.3 3.0 copy-start.3
  149.3 3.0 copy-start.4
  149.3 3.0 copy-start.5
  151.4 1.0 copy-start.2
  195.8 3.0 copy-start.3
  195.8 3.0 copy-start.4
  195.8 3.0 copy-start.5
  197.9 1.0 copy-start.2
  242.3 3.0 copy-start.3
  242.3 3.0 copy-start.4
  242.3 3.0 copy-start.5
  244.4 1.0 copy-start.2
  288.8 3.0 copy-start.3
  288.8 3.0 copy-start.4
  288.8 3.0 copy-start.5
  290.9 1.0 copy-start.2
  324.7 21.6 %collective-permute-start.5 = (bf16[2048,256]{1,0:T(8,128)(2,1)S(1)}, bf16[2048,256]{1,0:T(8,128)(2,1)S(1)}, u32[]{:S(2)}, u32[]{:S(2)}) collective-permute-start(bf16[2048,256]{1,0:T(8,128)(2,1)S(1)} %convert_element_type.104), channel_id=1, source_target_pairs={{0,8},{8,0},{16,24},{24,16},{32,40},{40,32},{48,56},{56,48},{64,72... | collective-permute-start | bytes 3145736 | tf_op jit(solution)/shard_map/ppermute | solution.py:20
  346.6 205.8 %collective-permute-start.6 = (bf16[2048,256]{1,0:T(8,128)(2,1)S(1)}, bf16[2048,256]{1,0:T(8,128)(2,1)S(1)}, u32[]{:S(2)}, u32[]{:S(2)}) collective-permute-start(bf16[2048,256]{1,0:T(8,128)(2,1)S(1)} %fusion.7), channel_id=1, source_target_pairs={{0,16},{16,0},{8,24},{24,8},{32,48},{48,32},{40,56},{56,40},{64,80... | collective-permute-start | bytes 3145736 | tf_op jit(solution)/shard_map/ppermute | solution.py:20
  552.8 21.0 %collective-permute-start.7 = (bf16[2048,256]{1,0:T(8,128)(2,1)S(1)}, bf16[2048,256]{1,0:T(8,128)(2,1)S(1)}, u32[]{:S(2)}, u32[]{:S(2)}) collective-permute-start(bf16[2048,256]{1,0:T(8,128)(2,1)S(1)} %get-tuple-element.221), channel_id=1, source_target_pairs={{0,32},{32,0},{8,40},{40,8},{16,48},{48,16},{24,56},{56,24},{64,96... | collective-permute-start | bytes 3145736 | tf_op jit(solution)/shard_map/ppermute | solution.py:20
  574.0 38.6 %copy-start = (f32[2048,256]{1,0:T(8,128)S(1)}, f32[2048,256]{1,0:T(8,128)}, u32[]{:S(2)}) copy-start(f32[2048,256]{1,0:T(8,128)} %get-tuple-element.197) | copy-start | bytes 6291460
  574.0 20.0 %collective-permute-start.8 = (bf16[2048,256]{1,0:T(8,128)(2,1)S(1)}, bf16[2048,256]{1,0:T(8,128)(2,1)S(1)}, u32[]{:S(2)}, u32[]{:S(2)}) collective-permute-start(bf16[2048,256]{1,0:T(8,128)(2,1)S(1)} %fusion.8), channel_id=1, source_target_pairs={{0,64},{64,0},{8,72},{72,8},{16,80},{80,16},{24,88},{88,24},{32,96... | collective-permute-start | bytes 3145736 | tf_op jit(solution)/shard_map/ppermute | solution.py:20
  594.4 18.2 %collective-permute-start.9 = (bf16[2048,256]{1,0:T(8,128)(2,1)S(1)}, bf16[2048,256]{1,0:T(8,128)(2,1)S(1)}, u32[]{:S(2)}, u32[]{:S(2)}) collective-permute-start(bf16[2048,256]{1,0:T(8,128)(2,1)S(1)} %fusion.9), channel_id=1, source_target_pairs={{0,128},{128,0},{8,136},{136,8},{16,144},{144,16},{24,152},{152,24... | collective-permute-start | bytes 3145736 | tf_op jit(solution)/shard_map/ppermute | solution.py:20
  614.4 92.4 %copy-start.11 = (f32[2048]{0:T(1024)S(1)}, f32[2048]{0:T(1024)}, u32[]{:S(2)}) copy-start(f32[2048]{0:T(1024)} %param.16) | copy-start | bytes 24580
  614.4 93.0 %copy-start.7 = (bf16[2048,256]{1,0:T(8,128)(2,1)S(1)}, bf16[2048,256]{1,0:T(8,128)(2,1)}, u32[]{:S(2)}) copy-start(bf16[2048,256]{1,0:T(8,128)(2,1)} %param.14) | copy-start | bytes 3145732
  704.7 2.8 copy-start.8
Sparse Core Ops, SparseCore 0:
  614.6 90.0 all-reduce.1
where the time goes:
time: 720 us; the launch traced here: 716 us
  waiting for transfers between devices  298 us (41%)
  starting transfers between devices  197 us (27%)
  other arithmetic  96.4 us (13%)
  local copies, waits for them, and re-layouts  68.7 us (10%)
  matrix products  34.3 us (5%)
  between operations  15.5 us (2%)
    ppermute x10, waiting for transfers between devices, from_partner(): return lax.ppermute(block, axis, route)  208 us
    ppermute x10, starting transfers between devices, from_partner(): return lax.ppermute(block, axis, route)  197 us
    psum x1, waiting for transfers between devices, body(): summed = lax.psum(src_grad + returned, 'rep')  90.2 us
    scatter-add x8, other arithmetic, score_group(): grads_in[1].at[block_ids[2]].add(target_grad).at[block_negs]  47.5 us
    scatter-add x4, other arithmetic, score_group(): first = grads_in[0].at[block_ids[0]].add(source_grad)  25.6 us
    gather x4, local copies, waits for them, and re-layouts, group_terms(): negative_rows = jnp.take(dst_block, negative_ids, axis=0)  19.8 us
    gather x8, local copies, waits for them, and re-layouts, group_terms(): source_rows = jnp.take(src_block, src_ids, axis=0).astype(jnp.float32)  15.1 us
  transfers between devices with their start and end apart: 11, of which 11 were waited for; matrix products, arithmetic and copies ran while one was open for 0% of the time, Pallas kernels for 0%

commit v1 on v0

v1 whole, which is shorter than its diff:
```python
import jax
import jax.numpy as jnp
from jax import lax
from jax.experimental import pallas as pl
from jax.experimental.pallas import tpu as pltpu
from jax.sharding import PartitionSpec as P

LEARN_RATE = 0.1
ROOT_EPSILON = 1e-08
BLOCK = 512
CHUNK = 256
PIECES = 4
STAGES = 5
MESH = pl.DeviceIdType.MESH
NN = (((1,), (0,)), ((), ()))
NT = (((1,), (1,)), ((), ()))
BF = jnp.bfloat16
F32 = jnp.float32


def mul(a, b, dims):
    return lax.dot_general(a, b, dims, preferred_element_type=F32)


def turned(block):
    return block.astype(F32).T


def kernel(
    comm,
    matching, counts, codes, scales, accum, relations, edges, negatives,
    out_codes, out_accum,
    rows, src_t, query_t, rel_t, qg_t, g_t, hits, tall, rel_turned, spots,
    dg_acc, dg_own, sg_own, held2,
    xbuf, dg_mate_in, dg_far_in, dg_mate_out, dg_far_out,
    sg_mate_in, sg_far_in, sg_mate_out, sg_far_out,
    x_s, x_r, ag_s, ag_r, dm_s, dm_r, df_s, df_r, sm_s, sm_r, sf_s, sf_r, o_s, o_r,
):
    n_chunk = codes.shape[0] // CHUNK
    n_block = edges.shape[1] // BLOCK
    if comm:
        d = lax.axis_index("dom")
        r = lax.axis_index("rep")
    else:
        d = jnp.int32(0)
        r = jnp.int32(0)
    core = r % 2
    z_hi = r // 2
    mate = {"rep": r + 1 - 2 * core}

    def far(dz):
        return {"rep": ((z_hi + dz) % 4) * 2 + core}

    def chunk_of(dz, dc):
        return ((z_hi + dz) % 4) * 2 + (core if dc == 0 else 1 - core)

    near = [
        {"dom": d + 1 - 2 * (d % 2)},
        {"dom": d + 8 - 16 * ((d // 8) % 2)},
        {"dom": d + 3 - 2 * (d % 4)},
        {"dom": d + 24 - 16 * (d // 8)},
        {"dom": d + 4 - 8 * ((d // 4) % 2)},
    ]
    partner = jnp.bitwise_xor(matching[0], d)
    in_x = jnp.bitwise_and(partner, 3)
    in_z = jnp.bitwise_and(jnp.right_shift(partner, 2), 1)
    in_y = jnp.bitwise_and(jnp.right_shift(partner, 3), 3)
    wanted = [
        (in_x == 1) | (in_x == 2),
        (in_y == 1) | (in_y == 2),
        in_x >= 2,
        in_y >= 2,
        in_z == 1,
    ]
    wanted = [w.astype(F32) for w in wanted]

    def copy(src, dst, s, t, to):
        return pltpu.make_async_remote_copy(
            src_ref=src, dst_ref=dst, send_sem=s, recv_sem=t, device_id=to, device_id_type=MESH
        )

    def start(c):
        if comm:
            c.start()

    def got(c):
        if comm:
            c.wait_recv()

    def left(c):
        if comm:
            c.wait_send()

    if comm:
        barrier = pltpu.get_barrier_semaphore()
        for to in near + [mate, far(1), far(2), far(3)]:
            pl.semaphore_signal(barrier, inc=1, device_id=to, device_id_type=MESH)

    def piece_copy(which, held, j, p):
        part = held.at[pl.ds(p * (CHUNK // PIECES), CHUNK // PIECES)]
        st = (p + j) % STAGES
        return copy(part, xbuf.at[which, j, p], x_s.at[which, j, p], x_r.at[which, j, p], near[st])

    def start_round(which, held, j):
        for p in range(PIECES):
            start(piece_copy(which, held, j, p))

    def end_round(which, held, j):
        for p in range(PIECES):
            c = piece_copy(which, held, j, p)
            got(c)
            left(c)
            take = wanted[(p + j) % STAGES]
            part = pl.ds(p * (CHUNK // PIECES), CHUNK // PIECES)
            mine = held[part, :].astype(F32)
            theirs = xbuf[which, j, p].astype(F32)
            held[part, :] = jnp.where(
                jnp.full(mine.shape, take, F32) > 0.5, theirs, mine
            ).astype(BF)
            if j + 1 < STAGES:
                start(piece_copy(which, held, j + 1, p))

    def scale_row(k):
        return scales[:, pl.ds(pl.multiple_of(k * CHUNK, CHUNK), CHUNK)].astype(F32)

    def values_t(k):
        at = pl.multiple_of(k * CHUNK, CHUNK)
        return turned(codes[pl.ds(at, CHUNK), :]) * scale_row(k)

    rows[0] = values_t(r).T.astype(BF)
    if comm:
        pl.semaphore_wait(barrier, len(near) + 4)
    start_round(0, rows.at[0], 0)

    spots[...] = lax.broadcasted_iota(jnp.int32, spots.shape, 0).astype(F32).astype(BF)
    rel_turned[...] = turned(relations[...]).astype(BF)

    def tables(k, _):
        src_t[k] = values_t(k).astype(BF)
        return 0

    lax.fori_loop(0, n_chunk, tables, 0)

    def count_block(c, _):
        ids = negatives[pl.ds(c, 1), :]
        high = jnp.right_shift(ids, 8)
        low = jnp.bitwise_and(ids, CHUNK - 1)
        n = ids.shape[1]
        high_hot = jnp.where(
            lax.broadcasted_iota(jnp.int32, (n_chunk, n), 0) == high, 1.0, 0.0
        ).astype(BF)
        low_hot = jnp.where(
            lax.broadcasted_iota(jnp.int32, (CHUNK, n), 0) == low, 1.0, 0.0
        ).astype(BF)
        table = mul(high_hot, low_hot, NT) * (0.5 / n)
        for k in range(n_chunk):
            tall[...] = jnp.broadcast_to(table[k : k + 1, :], (128, CHUNK))
            hits[k, c] = tall[...].T.astype(BF)
        return 0

    lax.fori_loop(0, n_block, count_block, 0)

    def hot_rows(ids, k):
        local = jnp.where(jnp.right_shift(ids, 8) == k, jnp.bitwise_and(ids, CHUNK - 1), -1)
        local = local.astype(F32).astype(BF)
        return spots[...] == local

    one, zero = jnp.ones((), BF), jnp.zeros((), BF)

    def query_block(c, _):
        at = pl.ds(pl.multiple_of(c * BLOCK, BLOCK), BLOCK)
        src = edges[0:1, at]
        slot = lax.broadcasted_iota(jnp.int32, (1, BLOCK), 1) + c * BLOCK
        rel = jnp.where(slot < counts[0], edges[1:2, at], -1)
        n_rel = relations.shape[0]
        rel_hot = jnp.where(
            lax.broadcasted_iota(jnp.int32, (n_rel, BLOCK), 0) == rel, 1.0, 0.0
        ).astype(BF)
        rel_rows = mul(rel_turned[...], rel_hot, NN)
        found = jnp.zeros((CHUNK, BLOCK), F32)
        for k in range(n_chunk):
            found = found + mul(src_t[k], jnp.where(hot_rows(src, k), one, zero), NN)
        query_t[:, at] = (found * rel_rows).astype(BF)
        rel_t[:, at] = rel_rows.astype(BF)
        qg_t[:, at] = jnp.zeros((CHUNK, BLOCK), F32)
        return 0

    per = n_block // 4
    for j in range(4):
        lax.fori_loop(j * per, (j + 1) * per, query_block, 0)
        end_round(0, rows.at[0], j)
    end_round(0, rows.at[0], 4)

    ag = {}
    ag[1] = copy(rows.at[0], rows.at[1], ag_s.at[0], ag_r.at[1], mate)
    start(ag[1])
    for dz in (1, 3, 2):
        back = (4 - dz) % 4
        ag[2 * back] = copy(rows.at[0], rows.at[2 * back], ag_s.at[dz], ag_r.at[2 * back], far(dz))
        start(ag[2 * back])

    def relay(dz):
        got(ag[2 * dz])
        ag[2 * dz + 1] = copy(
            rows.at[2 * dz], rows.at[2 * dz + 1], ag_s.at[3 + dz], ag_r.at[2 * dz + 1], mate
        )
        start(ag[2 * dz + 1])

    def score_chunk(slot, k):
        there = rows[slot]
        half = there * jnp.asarray(0.5, BF)
        there_t = turned(there).astype(BF)
        dg_acc[...] = jnp.zeros_like(dg_acc)

        def block(c, _):
            at = pl.ds(pl.multiple_of(c * BLOCK, BLOCK), BLOCK)
            query = query_t[:, at]
            t = jnp.tanh(mul(half, query, NN))
            up = (t + 1.0).astype(BF)
            down = (t * 0.5 - 0.5).astype(BF)
            often = hits[k, c]
            neg = jnp.concatenate([often] * (BLOCK // 128), axis=1) * up
            coef = jnp.where(hot_rows(edges[2:3, at], k), neg + down, neg)
            qg_t[:, at] += mul(there_t, coef, NN)
            dg_acc[...] += mul(coef, query, NT)
            return 0

        lax.fori_loop(0, n_block, block, 0, unroll=2)
        return dg_acc[...]

    def reduce_pair(dz, run, own, mate_in, far_in, mate_out, far_out, m_s, m_r, f_s, f_r):
        to_mate = copy(mate_out.at[dz], mate_in.at[dz], m_s.at[dz], m_r.at[dz], mate)
        if dz == 0:
            own[...] = run(0, 0)
            mate_out[0] = run(0, 1).astype(BF)
            start(to_mate)
            return [to_mate]
        mate_out[dz] = run(dz, 1).astype(BF)
        start(to_mate)
        both = run(dz, 0)
        got(to_mate)
        far_out[dz - 1] = (both + mate_in[dz].astype(F32)).astype(BF)
        back = (4 - dz) % 4
        away = copy(far_out.at[dz - 1], far_in.at[back - 1], f_s.at[dz - 1], f_r.at[back - 1], far(dz))
        start(away)
        return [to_mate, away]

    def total(own, mate_in, far_in):
        whole = own[...] + mate_in[0].astype(F32)
        for j in range(3):
            whole = whole + far_in[j].astype(F32)
        return whole

    dg_refs = (dg_own, dg_mate_in, dg_far_in, dg_mate_out, dg_far_out, dm_s, dm_r, df_s, df_r)
    sg_refs = (sg_own, sg_mate_in, sg_far_in, sg_mate_out, sg_far_out, sm_s, sm_r, sf_s, sf_r)
    sent = []

    def run_scores(dz, dc):
        if dc == 1:
            got(ag[2 * dz + 1])
        return score_chunk(2 * dz + dc, chunk_of(dz, dc))

    dg_copies = {}
    for i, dz in enumerate((0, 1, 3, 2)):
        dg_copies[dz] = reduce_pair(dz, run_scores, *dg_refs)
        if i == 0:
            for other in (1, 3, 2):
                relay(other)

    def finish_query_grad(c, _):
        at = pl.ds(pl.multiple_of(c * BLOCK, BLOCK), BLOCK)
        g_t[:, at] = (qg_t[:, at] * rel_t[:, at].astype(F32)).astype(BF)
        return 0

    lax.fori_loop(0, n_block, finish_query_grad, 0)

    def run_source(dz, dc):
        k = chunk_of(dz, dc)
        dg_acc[...] = jnp.zeros_like(dg_acc)

        def block(c, _):
            at = pl.ds(pl.multiple_of(c * BLOCK, BLOCK), BLOCK)
            hot = jnp.where(hot_rows(edges[0:1, at], k), one, zero)
            dg_acc[...] += mul(hot, g_t[:, at], NT)
            return 0

        lax.fori_loop(0, n_block, block, 0, unroll=4)
        return dg_acc[...]

    sg_copies = {}
    for dz in (2, 1):
        sg_copies[dz] = reduce_pair(dz, run_source, *sg_refs)

    got(dg_copies[0][0])
    for dz in (1, 2, 3):
        got(dg_copies[dz][1])
    held2[...] = total(dg_own, dg_mate_in, dg_far_in).astype(BF)
    start_round(1, held2, 0)
    sg_copies[3] = reduce_pair(3, run_source, *sg_refs)
    end_round(1, held2, 0)
    sg_copies[0] = reduce_pair(0, run_source, *sg_refs)
    for j in range(1, STAGES):
        end_round(1, held2, j)

    got(sg_copies[0][0])
    for dz in (1, 2, 3):
        got(sg_copies[dz][1])
    grad_t = turned(total(sg_own, sg_mate_in, sg_far_in) + held2[...].astype(F32))
    here = pl.ds(pl.multiple_of(r * CHUNK, CHUNK), CHUNK)
    state = accum[:, here] + jnp.mean(grad_t * grad_t, axis=0, keepdims=True)
    out_accum[...] = state
    updated = values_t(r) - LEARN_RATE * grad_t / (jnp.sqrt(state) + ROOT_EPSILON)
    out_codes[here, :] = (updated / scale_row(r)).T.astype(BF)

    mine = out_codes.at[here]
    og = {1: copy(mine, mine, o_s.at[0], o_r.at[1], mate)}
    start(og[1])
    for dz in (2, 1, 3):
        back = (4 - dz) % 4
        og[2 * back] = copy(mine, mine, o_s.at[dz], o_r.at[2 * back], far(dz))
        start(og[2 * back])
    for dz in (1, 3, 2):
        got(og[2 * dz])
        theirs = out_codes.at[pl.ds(pl.multiple_of(chunk_of(dz, 0) * CHUNK, CHUNK), CHUNK)]
        og[2 * dz + 1] = copy(theirs, theirs, o_s.at[3 + dz], o_r.at[2 * dz + 1], mate)
        start(og[2 * dz + 1])
    for dc in (1, 3, 5, 7):
        got(og[dc])
    for c in list(og.values()) + list(ag.values()):
        left(c)
    for copies in list(dg_copies.values()) + list(sg_copies.values()):
        for c in copies:
            left(c)
    for c in sent:
        left(c)


def call(comm, matching, counts, codes, scales, accum, relations, edges, negatives):
    import functools

    n, width = codes.shape
    slots = edges.shape[1]
    n_chunk, n_block = n // CHUNK, slots // BLOCK
    share = (CHUNK, width)
    vmem = pl.BlockSpec(memory_space=pltpu.VMEM)
    smem = pl.BlockSpec(memory_space=pltpu.SMEM)
    sem = pltpu.SemaphoreType.DMA
    scratch = [
        pltpu.VMEM((n_chunk,) + share, BF),
        pltpu.VMEM((n_chunk, width, CHUNK), BF),
        pltpu.VMEM((width, slots), BF),
        pltpu.VMEM((width, slots), BF),
        pltpu.VMEM((width, slots), F32),
        pltpu.VMEM((width, slots), BF),
        pltpu.VMEM((n_chunk, n_block, CHUNK, 128), BF),
        pltpu.VMEM((128, CHUNK), F32),
        pltpu.VMEM((width, relations.shape[0]), BF),
        pltpu.VMEM((CHUNK, BLOCK), BF),
        pltpu.VMEM(share, F32),
        pltpu.VMEM(share, F32),
        pltpu.VMEM(share, F32),
        pltpu.VMEM(share, BF),
        pltpu.VMEM((2, STAGES, PIECES, CHUNK // PIECES, width), BF),
    ]
    for _ in range(2):
        scratch += [pltpu.VMEM((4,) + share, BF), pltpu.VMEM((3,) + share, BF)] * 2
    scratch += [sem((2, STAGES, PIECES)), sem((2, STAGES, PIECES)), sem((7,)), sem((8,))]
    scratch += [sem((4,)), sem((4,)), sem((3,)), sem((3,))] * 2
    scratch += [sem((7,)), sem((8,))]
    return pl.pallas_call(
        functools.partial(kernel, comm),
        out_shape=(
            jax.ShapeDtypeStruct((n, width), BF),
            jax.ShapeDtypeStruct((1, CHUNK), F32),
        ),
        in_specs=[smem, smem] + [vmem] * 6,
        out_specs=(vmem, vmem),
        scratch_shapes=scratch,
        compiler_params=pltpu.CompilerParams(
            collective_id=0 if comm else None,
            has_side_effects=True,
            vmem_limit_bytes=48 << 20,
        ),
    )(
        matching, counts, codes, scales.reshape(1, n), accum.reshape(1, n), relations, edges,
        negatives,
    )


def body(codes, scales, accum, relations, matching, edges, counts, negatives):
    new_codes, new_accum = call(
        True, matching, counts, codes, scales, accum, relations, edges, negatives
    )
    return new_codes, new_accum.reshape(-1)


def solution(mesh):
    placed = (
        P("dom", None),
        P("dom"),
        P("dom"),
        P(),
        P("dom"),
        P(None, ("dom", "rep")),
        P(("dom", "rep")),
        P(("dom", "rep"), None),
    )
    return jax.shard_map(
        body,
        mesh=mesh,
        in_specs=placed,
        out_specs=(P("dom", None), P(("dom", "rep"))),
        check_vma=False,
    )
```

time: 720 us -> 115 us (0.16)
  waiting for transfers between devices: 298 us -> 0 us
  starting transfers between devices: 197 us -> 0 us
  Pallas kernels: 0 us -> 107 us
  other arithmetic: 96.4 us -> 0 us
  local copies, waits for them, and re-layouts: 68.7 us -> 5.13 us
  matrix products: 34.3 us -> 0 us
  between operations: 15.5 us -> 2.01 us
    ppermute x10 -> x0, waiting for transfers between devices: 208 us -> none  [from_partner(): return lax.ppermute(block, axis, route)]
    ppermute x10 -> x0, starting transfers between devices: 197 us -> none  [from_partner(): return lax.ppermute(block, axis, route)]
    pallas_call x0 -> x1, Pallas kernels: none -> 107 us  [call(): pl.pallas_call(functools.partial(kernel, comm), out_shape=(jax.ShapeDtype...]
    psum x1 -> x0, waiting for transfers between devices: 90.2 us -> none  [body(): summed = lax.psum(src_grad + returned, 'rep')]
    scatter-add x12 -> x0, other arithmetic: 73.1 us -> none  [the longest x8 47.5 us: score_group(): grads_in[1].at[block_ids[2]].add(target_grad).at[block_negs]]
    gather x20 -> x0, local copies, waits for them, and re-layouts: 46.1 us -> none  [the longest x4 19.8 us: group_terms(): negative_rows = jnp.take(dst_block, negative_ids, axis=0)]
    dot_general x16 -> x0, matrix products: 34.3 us -> none  [the longest x4 10.9 us: group_terms(): lax.dot_general(neg_coef, query, (((0,), (0,)), ((), ())), preferred_elem...]
    mul x8 -> x0, local copies, waits for them, and re-layouts: 16.3 us -> none  [the longest x4 8.17 us: group_terms(): source_grad = query_grad * relation_rows]
  transfers between devices with their start and end apart: 11 -> 0, of which waited for: 11 -> 0; matrix products, arithmetic and copies ran while one was open for 0% -> 0% of each run, Pallas kernels for 0% -> 0%
where the time goes in v1:
time: 115 us; the launch traced here: 114 us
  Pallas kernels  107 us (93%)
  local copies, waits for them, and re-layouts  5.13 us (4%)
  between operations  2.01 us (2%)
    pallas_call x1, Pallas kernels, call(): pl.pallas_call(functools.partial(kernel, comm), out_shape=(jax.ShapeDtype...  107 us
    unnamed x14, local copies, waits for them, and re-layouts  5.12 us

profile of v1, /device:TPU:1, one launch (start us, length us, event | category | flops | bytes accessed | tf_op | source)
XLA Modules:
  0.0 114.3 jit_solution(11707137235197217789)
XLA Ops:
  0.6 0.0 copy-start.5
  1.3 0.0 copy-start.4
  2.0 0.0 copy-done.5
  2.0 0.0 copy-done.4
  2.0 0.0 copy-start
  2.0 1.2 %copy-done = bf16[2048,256]{1,0:T(8,128)(2,1)S(1)} copy-done((bf16[2048,256]{1,0:T(8,128)(2,1)S(1)}, bf16[2048,256]{1,0:T(8,128)(2,1)}, u32[]{:S(2)}) %copy-start) | copy-done | bytes 1048600
  3.2 0.0 copy-start.1
  3.2 0.8 copy-done.1
  4.1 0.0 copy-start.2
  4.1 0.8 copy-done.2
  4.8 0.0 copy-start.3
  4.8 0.8 copy-done.3
  5.6 107.1 %shard_map.95 = (bf16[2048,256]{1,0:T(8,128)(2,1)S(1)}, f32[1,256]{1,0:T(1,128)S(1)}) custom-call(s32[1]{0:T(128)S(6)} %copy.12.matching, s32[1]{0:T(128)S(6)} %copy.13.counts, bf16[2048,256]{1,0:T(8,128)(2,1)S(1)} %copy-done, bf16[1,2048]{1,0:T(2,128)(2,1)S(1)} %reshape.13.scales, f32[1,2048]{1,0:T(1,128)S(1)} %bitcast.2, bf16[64,256]{1,0:T(8,128)(2,1)S(1)} %copy-done.2, ...), custom_call_target="tpu_custom_call" | custom-call | tf_op jit(solution)/shard_map/pallas_call | solution.py:370
  112.7 1.0 copy.14
  113.7 0.6 copy.15
  (1 shorter events, 0.0 us)
Async XLA Ops:
  0.6 1.3 %copy-start.5 = (bf16[2048]{0:T(1024)(128)(2,1)S(1)}, bf16[2048]{0:T(1024)(128)(2,1)}, u32[]{:S(2)}) copy-start(bf16[2048]{0:T(1024)(128)(2,1)} %param.9) | copy-start | bytes 12292
  1.3 0.7 copy-start.4
  2.0 1.2 %copy-start = (bf16[2048,256]{1,0:T(8,128)(2,1)S(1)}, bf16[2048,256]{1,0:T(8,128)(2,1)}, u32[]{:S(2)}) copy-start(bf16[2048,256]{1,0:T(8,128)(2,1)} %codes.1) | copy-start | bytes 3145732
  3.2 0.8 copy-start.1
  4.1 0.8 copy-start.2
  4.8 0.8 copy-start.3

commit v2 on v0

v2 whole, which is shorter than its diff:
```python
import functools

import jax
import jax.numpy as jnp
from jax import lax
from jax.experimental import pallas as pl
from jax.experimental.pallas import tpu as pltpu
from jax.sharding import PartitionSpec as P

LEARN_RATE = 0.1
ROOT_EPSILON = 1e-08
BLOCK = 512
CHUNK = 256
PIECES = ((0, 96), (96, 80), (176, 80))
MESH = pl.DeviceIdType.MESH
NN = (((1,), (0,)), ((), ()))
NT = (((1,), (1,)), ((), ()))
BF = jnp.bfloat16
F32 = jnp.float32


def mul(a, b, dims):
    return lax.dot_general(a, b, dims, preferred_element_type=F32)


def turned(block):
    return block.astype(F32).T


def kernel(
    comm,
    matching, counts, codes_hbm, scales_hbm, accum_hbm, relations_hbm, edges_hbm, negatives_hbm,
    out_codes, out_accum,
    share, codes, scales, accum, relations, edges, negatives,
    rows, rows_t, src_t, query_t, rel_t, g_t, coefs, hits, rel_turned, spots, spread,
    score_a, score_b, acc, dg_own, sg_own, held,
    xbuf, dg_mate_in, dg_far_in, dg_mate_out, dg_far_out,
    sg_mate_in, sg_far_in, sg_mate_out, sg_far_out,
    l_s, x_s, x_r, ag_s, ag_r, dm_s, dm_r, df_s, df_r, sm_s, sm_r, sf_s, sf_r, o_s, o_r,
):
    n_chunk = codes.shape[0] // CHUNK
    n_block = edges.shape[1] // BLOCK
    if comm:
        d = lax.axis_index("dom")
        r = lax.axis_index("rep")
    else:
        d = jnp.int32(0)
        r = jnp.int32(0)
    core = r % 2
    z_hi = r // 2
    mate = {"rep": r + 1 - 2 * core}

    def far(dz):
        return {"rep": ((z_hi + dz) % 4) * 2 + core}

    def pair_of(dz):
        return (z_hi + dz) % 4

    def span(i, n):
        return pl.ds(pl.multiple_of(i * n, n), n)

    near_x = [
        {"dom": d + 1 - 2 * (d % 2)},
        {"dom": d + 2 - 4 * ((d // 2) % 2)},
        {"dom": d + 3 - 2 * (d % 4)},
    ]
    near_z = [{"dom": d + 4 - 8 * ((d // 4) % 2)}]
    near_y = [
        {"dom": d + 8 - 16 * ((d // 8) % 2)},
        {"dom": d + 16 - 32 * ((d // 16) % 2)},
        {"dom": d + 24 - 16 * (d // 8)},
    ]
    partner = jnp.bitwise_xor(matching[0], d)
    in_x = jnp.bitwise_and(partner, 3)
    in_z = jnp.bitwise_and(jnp.right_shift(partner, 2), 1)
    in_y = jnp.bitwise_and(jnp.right_shift(partner, 3), 3)
    near = (near_y, near_x, near_z)
    wanted = [[(bits == i + 1).astype(F32) for i in range(3)] for bits in (in_y, in_x, in_z)]

    def copy(src, dst, s, t, to):
        return pltpu.make_async_remote_copy(
            src_ref=src, dst_ref=dst, send_sem=s, recv_sem=t, device_id=to, device_id_type=MESH
        )

    def start(*copies):
        if comm:
            for c in copies:
                c.start()

    def got(*copies):
        if comm:
            for c in copies:
                c.wait_recv()

    def left(*copies):
        if comm:
            for c in copies:
                c.wait_send()

    loads = [
        pltpu.make_async_copy(a, b, l_s.at[i])
        for i, (a, b) in enumerate(
            (
                (codes_hbm.at[span(r, CHUNK)], share),
                (scales_hbm, scales),
                (codes_hbm, codes),
                (relations_hbm, relations),
                (negatives_hbm, negatives),
                (edges_hbm, edges),
                (accum_hbm, accum),
            )
        )
    ]
    for c in loads:
        c.start()
    if comm:
        barrier = pltpu.get_barrier_semaphore()
        peers = near_x + near_y + near_z + [mate, far(1), far(2), far(3)]
        for to in peers:
            pl.semaphore_signal(barrier, inc=1, device_id=to, device_id_type=MESH)

    def piece_copies(which, j, p):
        at, n = PIECES[p]
        dim = (p + j) % 3
        return [
            copy(
                held.at[which, pl.ds(at, n)], xbuf.at[which, j, i, pl.ds(at, n)],
                x_s.at[which, j, p, i], x_r.at[which, j, p, i], to,
            )
            for i, to in enumerate(near[dim])
        ]

    def start_round(which, j):
        for p in range(3):
            start(*piece_copies(which, j, p))

    def end_round(which, j):
        for p, (at, n) in enumerate(PIECES):
            copies = piece_copies(which, j, p)
            got(*copies)
            left(*copies)
            kept = held[which, at : at + n, :].astype(F32)
            for i in range(len(copies)):
                take = jnp.full(kept.shape, wanted[(p + j) % 3][i], F32) > 0.5
                kept = jnp.where(take, xbuf[which, j, i, at : at + n, :].astype(F32), kept)
            held[which, at : at + n, :] = kept.astype(BF)
            if j < 2:
                start(*piece_copies(which, j + 1, p))

    def gather(slot, s, t, fixed=False):
        top, low = 0, CHUNK // 2

        def part(dz, at):
            return slot(dz, at, CHUNK // 2)

        def whole(dz):
            return slot(dz, 0, CHUNK)

        c = {}
        c["m0"] = copy(whole(0), whole(0), s.at[0], t.at[0], mate)
        c["a1t"] = copy(part(0, top), part(0, top) if fixed else part(3, top), s.at[1], t.at[1], far(1))
        c["a3b"] = copy(part(0, low), part(0, low) if fixed else part(1, low), s.at[2], t.at[2], far(3))
        c["a1b"] = copy(part(0, low), part(0, low) if fixed else part(3, low), s.at[3], t.at[3], far(1))
        c["a3t"] = copy(part(0, top), part(0, top) if fixed else part(1, top), s.at[4], t.at[4], far(3))
        c["f1"] = copy(part(3, top), part(3, top) if fixed else part(2, top), s.at[5], t.at[5], far(1))
        c["f3"] = copy(part(1, low), part(1, low) if fixed else part(2, low), s.at[6], t.at[6], far(3))
        for i, dz in enumerate((1, 3, 2)):
            c["m%d" % dz] = copy(whole(dz), whole(dz), s.at[7 + i], t.at[7 + i], mate)
        return c

    def gather_start(c):
        start(c["a1t"], c["a3b"], c["a1b"], c["a3t"], c["m0"])

    def gather_forward(c):
        got(c["a1t"])
        start(c["f1"])
        got(c["a3b"])
        start(c["f3"])

    def gather_mate(c):
        got(c["a3t"])
        start(c["m1"])
        got(c["a1b"])
        start(c["m3"])

    def gather_last(c):
        got(c["f1"], c["f3"])
        start(c["m2"])

    def scale_row(k):
        return scales[:, span(k, CHUNK)].astype(F32)

    loads[0].wait()
    loads[1].wait()
    share_t = turned(share[...]) * scale_row(r)
    held[0] = share_t.T.astype(BF)
    if comm:
        pl.semaphore_wait(barrier, len(peers))
    start_round(0, 0)

    for c in loads[2:]:
        c.wait()
    spots[...] = lax.broadcasted_iota(jnp.int32, spots.shape, 0).astype(F32).astype(BF)
    spread[...] = jnp.where(
        lax.broadcasted_iota(jnp.int32, spread.shape, 0)
        == jnp.right_shift(lax.broadcasted_iota(jnp.int32, spread.shape, 1), 7),
        1.0,
        0.0,
    ).astype(BF)
    rel_turned[...] = turned(relations[...]).astype(BF)
    one, zero = jnp.ones((), BF), jnp.zeros((), BF)

    def tables(k, _):
        src_t[k] = (turned(codes[span(k, CHUNK), :]) * scale_row(k)).astype(BF)
        return 0

    def count_block(c, _):
        ids = negatives[pl.ds(c, 1), :]
        n = ids.shape[1]
        low = jnp.bitwise_and(ids, CHUNK - 1).astype(F32).astype(BF)
        low_hot = jnp.where(spots[...] == low, one, zero)
        high_hot = jnp.where(
            lax.broadcasted_iota(jnp.int32, (128, n), 0) == jnp.right_shift(ids, 8), 1.0, 0.0
        ).astype(BF)
        table = (mul(low_hot, high_hot, NT) * (1.0 / n)).astype(BF)
        hits[c] = mul(table, spread[...], NN).astype(BF)
        return 0

    def hot_rows(ids, k):
        local = jnp.where(jnp.right_shift(ids, 8) == k, jnp.bitwise_and(ids, CHUNK - 1), -1)
        return spots[:, 0:BLOCK] == local.astype(F32).astype(BF)

    def query_block(c, _):
        at = span(c, BLOCK)
        src = edges[0:1, at]
        slot = lax.broadcasted_iota(jnp.int32, (1, BLOCK), 1) + c * BLOCK
        rel = jnp.where(slot < counts[0], edges[1:2, at], -1)
        n_rel = relations.shape[0]
        rel_hot = jnp.where(
            lax.broadcasted_iota(jnp.int32, (n_rel, BLOCK), 0) == rel, 1.0, 0.0
        ).astype(BF)
        rel_rows = mul(rel_turned[...], rel_hot, NN)
        found = jnp.zeros((CHUNK, BLOCK), F32)
        for k in range(n_chunk):
            found = found + mul(src_t[k], jnp.where(hot_rows(src, k), one, zero), NN)
        query_t[:, at] = (found * rel_rows).astype(BF)
        rel_t[:, at] = (rel_rows * 0.5).astype(BF)
        return 0

    lax.fori_loop(0, n_chunk, tables, 0, unroll=8)
    lax.fori_loop(0, n_block // 2, count_block, 0, unroll=4)
    end_round(0, 0)
    lax.fori_loop(n_block // 2, n_block, count_block, 0, unroll=4)
    end_round(0, 1)
    lax.fori_loop(0, n_block // 4, query_block, 0, unroll=2)
    end_round(0, 2)
    rows[0, span(core, CHUNK)] = held[0]

    def row_slot(dz, at, n):
        return rows.at[dz, pl.ds(pl.multiple_of(core * CHUNK + at, n), n)]

    ag = gather(row_slot, ag_s, ag_r)
    gather_start(ag)
    lax.fori_loop(n_block // 4, 3 * n_block // 4, query_block, 0, unroll=2)
    gather_forward(ag)
    lax.fori_loop(3 * n_block // 4, n_block, query_block, 0, unroll=2)

    def score_pair(dz):
        a = pair_of(dz)
        there = rows[dz]
        rows_t[dz] = turned(there).astype(BF)
        half = there * jnp.asarray(0.5, BF)
        acc[...] = jnp.zeros_like(acc)

        def score(c):
            return mul(half, query_t[:, span(c, BLOCK)], NN)

        def use(c, scores):
            at = span(c, BLOCK)
            dst = edges[2:3, at]
            for h in range(2):
                k = 2 * a + h
                t = jnp.tanh(scores[h * CHUNK : (h + 1) * CHUNK, :])
                up = (t + 1.0).astype(BF)
                down = (t - 1.0).astype(BF)
                often = hits[c, :, span(k, 128)]
                neg = jnp.concatenate([often] * (BLOCK // 128), axis=1) * up
                coefs[dz, h * CHUNK : (h + 1) * CHUNK, at] = jnp.where(
                    hot_rows(dst, k), neg + down, neg
                )
            acc[...] += mul(coefs[dz, :, at], query_t[:, at], NT)

        def two(i, _):
            score_b[...] = score(2 * i + 1)
            use(2 * i, score_a)
            score_a[...] = score(2 * i + 2)
            use(2 * i + 1, score_b)
            return 0

        score_a[...] = score(0)
        lax.fori_loop(0, n_block // 2 - 1, two, 0, unroll=3)
        score_b[...] = score(n_block - 1)
        use(n_block - 2, score_a)
        use(n_block - 1, score_b)

    def source_pair(dz):
        a = pair_of(dz)
        acc[...] = jnp.zeros_like(acc)

        def block(c, _):
            at = span(c, BLOCK)
            src = edges[0:1, at]
            hot = jnp.concatenate(
                [jnp.where(hot_rows(src, 2 * a + h), one, zero) for h in range(2)], axis=0
            )
            acc[...] += mul(hot, g_t[:, at], NT)
            return 0

        lax.fori_loop(0, n_block, block, 0, unroll=8)

    class Reduce:
        def __init__(self, own, mate_in, far_in, mate_out, far_out, m_s, m_r, f_s, f_r):
            self.own, self.mate_in, self.far_in = own, mate_in, far_in
            self.mate_out, self.far_out = mate_out, far_out
            self.m = [
                copy(mate_out.at[dz], mate_in.at[dz], m_s.at[dz], m_r.at[dz], mate)
                for dz in range(4)
            ]
            self.f = [None] + [
                copy(far_out.at[dz - 1], far_in.at[3 - dz], f_s.at[dz - 1], f_r.at[3 - dz], far(dz))
                for dz in (1, 2, 3)
            ]

        def give(self, dz):
            self.mate_out[dz] = acc[span(1 - core, CHUNK), :].astype(BF)
            start(self.m[dz])
            self.own[dz] = acc[span(core, CHUNK), :]

        def send(self, dz):
            got(self.m[dz])
            self.far_out[dz - 1] = (self.own[dz] + self.mate_in[dz].astype(F32)).astype(BF)
            start(self.f[dz])

        def total(self):
            got(self.m[0], *self.f[1:])
            whole = self.own[0] + self.mate_in[0].astype(F32)
            for j in range(3):
                whole = whole + self.far_in[j].astype(F32)
            return whole

        def done(self):
            left(*self.m, *self.f[1:])

    dg = Reduce(dg_own, dg_mate_in, dg_far_in, dg_mate_out, dg_far_out, dm_s, dm_r, df_s, df_r)
    sg = Reduce(sg_own, sg_mate_in, sg_far_in, sg_mate_out, sg_far_out, sm_s, sm_r, sf_s, sf_r)

    got(ag["m0"])
    score_pair(0)
    dg.give(0)
    gather_mate(ag)
    got(ag["m1"])
    score_pair(1)
    dg.give(1)
    gather_last(ag)
    got(ag["m2"])
    score_pair(2)
    dg.give(2)
    dg.send(1)
    got(ag["m3"])
    score_pair(3)
    dg.give(3)
    dg.send(2)

    def query_grad(c, _):
        at = span(c, BLOCK)
        whole = jnp.zeros((CHUNK, BLOCK), F32)
        for dz in range(4):
            whole = whole + mul(rows_t[dz], coefs[dz, :, at], NN)
        g_t[:, at] = (whole * rel_t[:, at].astype(F32)).astype(BF)
        return 0

    lax.fori_loop(0, n_block // 4, query_grad, 0, unroll=2)
    dg.send(3)
    lax.fori_loop(n_block // 4, n_block, query_grad, 0, unroll=2)
    source_pair(2)
    sg.give(2)
    source_pair(1)
    sg.give(1)
    sg.send(2)
    held[1] = (dg.total() * 0.5).astype(BF)
    start_round(1, 0)
    source_pair(3)
    sg.give(3)
    sg.send(1)
    source_pair(0)
    sg.give(0)
    sg.send(3)
    for j in range(3):
        end_round(1, j)

    grad_t = (sg.total() + held[1].astype(F32)).T
    state = accum[:, span(r, CHUNK)] + jnp.mean(grad_t * grad_t, axis=0, keepdims=True)
    out_accum[...] = state
    values_t = turned(share[...]) * scale_row(r)
    updated = values_t - LEARN_RATE * grad_t / (jnp.sqrt(state) + ROOT_EPSILON)
    out_codes[span(r, CHUNK), :] = (updated / scale_row(r)).T.astype(BF)

    def out_slot(dz, at, n):
        return out_codes.at[pl.ds(pl.multiple_of((pair_of(dz) * 2 + core) * CHUNK + at, n), n)]

    og = gather(out_slot, o_s, o_r, True)
    gather_start(og)
    gather_forward(og)
    gather_mate(og)
    gather_last(og)
    got(og["m0"], og["m1"], og["m3"], og["m2"])
    left(*og.values(), *ag.values())
    dg.done()
    sg.done()


def call(comm, matching, counts, codes, scales, accum, relations, edges, negatives):
    n, width = codes.shape
    slots = edges.shape[1]
    n_chunk, n_block = n // CHUNK, slots // BLOCK
    n_neg = negatives.shape[1]
    one = (CHUNK, width)
    vmem = pl.BlockSpec(memory_space=pltpu.VMEM)
    smem = pl.BlockSpec(memory_space=pltpu.SMEM)
    hbm = pl.BlockSpec(memory_space=pl.ANY)
    sem = pltpu.SemaphoreType.DMA
    scratch = [
        pltpu.VMEM(one, BF),
        pltpu.VMEM((n, width), BF),
        pltpu.VMEM((1, n), BF),
        pltpu.VMEM((1, n), F32),
        pltpu.VMEM(relations.shape, BF),
        pltpu.VMEM(edges.shape, jnp.int32),
        pltpu.VMEM(negatives.shape, jnp.int32),
        pltpu.VMEM((4, 2 * CHUNK, width), BF),
        pltpu.VMEM((4, width, 2 * CHUNK), BF),
        pltpu.VMEM((n_chunk, width, CHUNK), BF),
        pltpu.VMEM((width, slots), BF),
        pltpu.VMEM((width, slots), BF),
        pltpu.VMEM((width, slots), BF),
        pltpu.VMEM((4, 2 * CHUNK, slots), BF),
        pltpu.VMEM((n_block, CHUNK, n_chunk * 128), BF),
        pltpu.VMEM((width, relations.shape[0]), BF),
        pltpu.VMEM((CHUNK, n_neg), BF),
        pltpu.VMEM((128, n_chunk * 128), BF),
        pltpu.VMEM((2 * CHUNK, BLOCK), F32),
        pltpu.VMEM((2 * CHUNK, BLOCK), F32),
        pltpu.VMEM((2 * CHUNK, width), F32),
        pltpu.VMEM((4,) + one, F32),
        pltpu.VMEM((4,) + one, F32),
        pltpu.VMEM((2,) + one, BF),
        pltpu.VMEM((2, 3, 3) + one, BF),
    ]
    for _ in range(2):
        scratch += [pltpu.VMEM((4,) + one, BF), pltpu.VMEM((3,) + one, BF)] * 2
    scratch += [sem((7,)), sem((2, 3, 3, 3)), sem((2, 3, 3, 3)), sem((10,)), sem((10,))]
    scratch += [sem((4,)), sem((4,)), sem((3,)), sem((3,))] * 2
    scratch += [sem((10,)), sem((10,))]
    return pl.pallas_call(
        functools.partial(kernel, comm),
        out_shape=(
            jax.ShapeDtypeStruct((n, width), BF),
            jax.ShapeDtypeStruct((1, CHUNK), F32),
        ),
        in_specs=[smem, smem] + [hbm] * 6,
        out_specs=(vmem, vmem),
        scratch_shapes=scratch,
        compiler_params=pltpu.CompilerParams(
            collective_id=0 if comm else None,
            has_side_effects=True,
            vmem_limit_bytes=50 << 20,
        ),
    )(
        matching, counts, codes, scales.reshape(1, n), accum.reshape(1, n), relations, edges,
        negatives,
    )


def body(codes, scales, accum, relations, matching, edges, counts, negatives):
    new_codes, new_accum = call(
        True, matching, counts, codes, scales, accum, relations, edges, negatives
    )
    return new_codes, new_accum.reshape(-1)


def solution(mesh):
    placed = (
        P("dom", None),
        P("dom"),
        P("dom"),
        P(),
        P("dom"),
        P(None, ("dom", "rep")),
        P(("dom", "rep")),
        P(("dom", "rep"), None),
    )
    return jax.shard_map(
        body,
        mesh=mesh,
        in_specs=placed,
        out_specs=(P("dom", None), P(("dom", "rep"))),
        check_vma=False,
    )
```

time: 720 us -> 99.4 us (0.14)
  waiting for transfers between devices: 298 us -> 0 us
  starting transfers between devices: 197 us -> 0 us
  other arithmetic: 96.4 us -> 0 us
  Pallas kernels: 0 us -> 91.9 us
  local copies, waits for them, and re-layouts: 68.7 us -> 5.13 us
  matrix products: 34.3 us -> 0 us
  between operations: 15.5 us -> 2.01 us
    ppermute x10 -> x0, waiting for transfers between devices: 208 us -> none  [from_partner(): return lax.ppermute(block, axis, route)]
    ppermute x10 -> x0, starting transfers between devices: 197 us -> none  [from_partner(): return lax.ppermute(block, axis, route)]
    pallas_call x0 -> x1, Pallas kernels: none -> 91.9 us  [call(): pl.pallas_call(functools.partial(kernel, comm), out_shape=(jax.ShapeDtype...]
    psum x1 -> x0, waiting for transfers between devices: 90.2 us -> none  [body(): summed = lax.psum(src_grad + returned, 'rep')]
    scatter-add x12 -> x0, other arithmetic: 73.1 us -> none  [the longest x8 47.5 us: score_group(): grads_in[1].at[block_ids[2]].add(target_grad).at[block_negs]]
    gather x20 -> x0, local copies, waits for them, and re-layouts: 46.1 us -> none  [the longest x4 19.8 us: group_terms(): negative_rows = jnp.take(dst_block, negative_ids, axis=0)]
    dot_general x16 -> x0, matrix products: 34.3 us -> none  [the longest x4 10.9 us: group_terms(): lax.dot_general(neg_coef, query, (((0,), (0,)), ((), ())), preferred_elem...]
    mul x8 -> x0, local copies, waits for them, and re-layouts: 16.3 us -> none  [the longest x4 8.17 us: group_terms(): source_grad = query_grad * relation_rows]
  transfers between devices with their start and end apart: 11 -> 0, of which waited for: 11 -> 0; matrix products, arithmetic and copies ran while one was open for 0% -> 0% of each run, Pallas kernels for 0% -> 0%
where the time goes in v2:
time: 99.4 us; the launch traced here: 99 us
  Pallas kernels  91.9 us (92%)
  local copies, waits for them, and re-layouts  5.13 us (5%)
  between operations  2.01 us (2%)
    pallas_call x1, Pallas kernels, call(): pl.pallas_call(functools.partial(kernel, comm), out_shape=(jax.ShapeDtype...  91.9 us
    unnamed x14, local copies, waits for them, and re-layouts  5.12 us

profile of v2, /device:TPU:1, one launch (start us, length us, event | category | flops | bytes accessed | tf_op | source)
XLA Modules:
  0.0 99.0 jit_solution(7176380582968787842)
XLA Ops:
  0.6 0.0 copy-start.5
  1.3 0.0 copy-start.4
  2.0 0.0 copy-done.5
  2.0 0.0 copy-done.4
  2.0 0.0 copy-start
  2.0 1.2 %copy-done = bf16[2048,256]{1,0:T(8,128)(2,1)S(1)} copy-done((bf16[2048,256]{1,0:T(8,128)(2,1)S(1)}, bf16[2048,256]{1,0:T(8,128)(2,1)}, u32[]{:S(2)}) %copy-start) | copy-done | bytes 1048600
  3.2 0.0 copy-start.1
  3.2 0.8 copy-done.1
  4.1 0.0 copy-start.2
  4.1 0.8 copy-done.2
  4.8 0.0 copy-start.3
  4.8 0.8 copy-done.3
  5.6 91.9 %shard_map.95 = (bf16[2048,256]{1,0:T(8,128)(2,1)S(1)}, f32[1,256]{1,0:T(1,128)S(1)}) custom-call(s32[1]{0:T(128)S(6)} %copy.12.matching, s32[1]{0:T(128)S(6)} %copy.13.counts, bf16[2048,256]{1,0:T(8,128)(2,1)S(1)} %copy-done, bf16[1,2048]{1,0:T(2,128)(2,1)S(1)} %reshape.13.scales_hbm, f32[1,2048]{1,0:T(1,128)S(1)} %bitcast.2, ...), custom_call_target="tpu_custom_call" | custom-call | tf_op jit(solution)/shard_map/pallas_call | solution.py:464
  97.5 1.0 copy.14
  98.4 0.6 copy.15
  (1 shorter events, 0.0 us)
Async XLA Ops:
  0.6 1.3 %copy-start.5 = (bf16[2048]{0:T(1024)(128)(2,1)S(1)}, bf16[2048]{0:T(1024)(128)(2,1)}, u32[]{:S(2)}) copy-start(bf16[2048]{0:T(1024)(128)(2,1)} %param.9) | copy-start | bytes 12292
  1.3 0.7 copy-start.4
  2.0 1.2 %copy-start = (bf16[2048,256]{1,0:T(8,128)(2,1)S(1)}, bf16[2048,256]{1,0:T(8,128)(2,1)}, u32[]{:S(2)}) copy-start(bf16[2048,256]{1,0:T(8,128)(2,1)} %codes_hbm.1) | copy-start | bytes 3145732
  3.2 0.8 copy-start.1
  4.1 0.8 copy-start.2
  4.8 0.8 copy-start.3

commit v3 on v2

--- a/solution.py
+++ b/solution.py
@@ -11,7 +11,8 @@
 ROOT_EPSILON = 1e-08
 BLOCK = 512
 CHUNK = 256
-PIECES = ((0, 96), (96, 80), (176, 80))
+PIECES = 4
+PIECE = CHUNK // PIECES
 MESH = pl.DeviceIdType.MESH
 NN = (((1,), (0,)), ((), ()))
 NT = (((1,), (1,)), ((), ()))
@@ -31,7 +32,7 @@
     comm,
     matching, counts, codes_hbm, scales_hbm, accum_hbm, relations_hbm, edges_hbm, negatives_hbm,
     out_codes, out_accum,
-    share, codes, scales, accum, relations, edges, negatives,
+    share, codes, scales, scale_col, accum_col, state_col, accum, relations, edges, negatives,
     rows, rows_t, src_t, query_t, rel_t, g_t, coefs, hits, rel_turned, spots, spread,
     score_a, score_b, acc, dg_own, sg_own, held,
     xbuf, dg_mate_in, dg_far_in, dg_mate_out, dg_far_out,
@@ -120,86 +121,85 @@
             pl.semaphore_signal(barrier, inc=1, device_id=to, device_id_type=MESH)
 
     def piece_copies(which, j, p):
-        at, n = PIECES[p]
-        dim = (p + j) % 3
+        at = pl.ds(p * PIECE, PIECE)
         return [
             copy(
-                held.at[which, pl.ds(at, n)], xbuf.at[which, j, i, pl.ds(at, n)],
+                held.at[which, at], xbuf.at[which, j, i, at],
                 x_s.at[which, j, p, i], x_r.at[which, j, p, i], to,
             )
-            for i, to in enumerate(near[dim])
+            for i, to in enumerate(near[order(j, p)])
         ]
 
-    def start_round(which, j):
-        for p in range(3):
-            start(*piece_copies(which, j, p))
-
-    def end_round(which, j):
-        for p, (at, n) in enumerate(PIECES):
+    def order(j, p):
+        return 2 if j == 2 else (p + j) % 2
+
+    def exchange_start(which):
+        for p in range(PIECES):
+            start(*piece_copies(which, 0, p))
+
+    def end_round(which, j, then=None):
+        for p in range(PIECES):
+            at = slice(p * PIECE, (p + 1) * PIECE)
             copies = piece_copies(which, j, p)
             got(*copies)
             left(*copies)
-            kept = held[which, at : at + n, :].astype(F32)
+            kept = held[which, at, :].astype(F32)
             for i in range(len(copies)):
-                take = jnp.full(kept.shape, wanted[(p + j) % 3][i], F32) > 0.5
-                kept = jnp.where(take, xbuf[which, j, i, at : at + n, :].astype(F32), kept)
-            held[which, at : at + n, :] = kept.astype(BF)
+                take = jnp.full(kept.shape, wanted[order(j, p)][i], F32) > 0.5
+                kept = jnp.where(take, xbuf[which, j, i, at, :].astype(F32), kept)
+            held[which, at, :] = kept.astype(BF)
             if j < 2:
                 start(*piece_copies(which, j + 1, p))
+            else:
+                then(p)
 
     def gather(slot, s, t, fixed=False):
-        top, low = 0, CHUNK // 2
-
-        def part(dz, at):
-            return slot(dz, at, CHUNK // 2)
+        def part(dz, p):
+            return slot(dz, p * PIECE, PIECE)
 
         def whole(dz):
             return slot(dz, 0, CHUNK)
 
         c = {}
-        c["m0"] = copy(whole(0), whole(0), s.at[0], t.at[0], mate)
-        c["a1t"] = copy(part(0, top), part(0, top) if fixed else part(3, top), s.at[1], t.at[1], far(1))
-        c["a3b"] = copy(part(0, low), part(0, low) if fixed else part(1, low), s.at[2], t.at[2], far(3))
-        c["a1b"] = copy(part(0, low), part(0, low) if fixed else part(3, low), s.at[3], t.at[3], far(1))
-        c["a3t"] = copy(part(0, top), part(0, top) if fixed else part(1, top), s.at[4], t.at[4], far(3))
-        c["f1"] = copy(part(3, top), part(3, top) if fixed else part(2, top), s.at[5], t.at[5], far(1))
-        c["f3"] = copy(part(1, low), part(1, low) if fixed else part(2, low), s.at[6], t.at[6], far(3))
-        for i, dz in enumerate((1, 3, 2)):
-            c["m%d" % dz] = copy(whole(dz), whole(dz), s.at[7 + i], t.at[7 + i], mate)
+        for p in range(PIECES):
+            mine = part(0, p)
+            c["up", p] = copy(mine, mine if fixed else part(3, p), s.at[p], t.at[p], far(1))
+            c["down", p] = copy(mine, mine if fixed else part(1, p), s.at[4 + p], t.at[4 + p], far(3))
+            c["mate", p] = copy(mine, mine, s.at[8 + p], t.at[8 + p], mate)
+            via, to = (3, far(1)) if p < PIECES // 2 else (1, far(3))
+            passing = part(via, p)
+            c["on", p] = copy(
+                passing, passing if fixed else part(2, p), s.at[12 + p], t.at[12 + p], to
+            )
+        for dz in (1, 2, 3):
+            c["relay", dz] = copy(whole(dz), whole(dz), s.at[15 + dz], t.at[15 + dz], mate)
         return c
 
-    def gather_start(c):
-        start(c["a1t"], c["a3b"], c["a1b"], c["a3t"], c["m0"])
+    def gather_piece(c, p):
+        start(c["up", p], c["down", p], c["mate", p])
 
     def gather_forward(c):
-        got(c["a1t"])
-        start(c["f1"])
-        got(c["a3b"])
-        start(c["f3"])
+        for p in range(PIECES):
+            got(c["up" if p < PIECES // 2 else "down", p])
+            start(c["on", p])
 
     def gather_mate(c):
-        got(c["a3t"])
-        start(c["m1"])
-        got(c["a1b"])
-        start(c["m3"])
+        got(*[c["down", p] for p in range(PIECES // 2)])
+        start(c["relay", 1])
+        got(*[c["up", p] for p in range(PIECES // 2, PIECES)])
+        start(c["relay", 3])
 
     def gather_last(c):
-        got(c["f1"], c["f3"])
-        start(c["m2"])
+        got(*[c["on", p] for p in range(PIECES)])
+        start(c["relay", 2])
 
     def scale_row(k):
         return scales[:, span(k, CHUNK)].astype(F32)
 
-    loads[0].wait()
-    loads[1].wait()
+    for c in loads:
+        c.wait()
     share_t = turned(share[...]) * scale_row(r)
     held[0] = share_t.T.astype(BF)
-    if comm:
-        pl.semaphore_wait(barrier, len(peers))
-    start_round(0, 0)
-
-    for c in loads[2:]:
-        c.wait()
     spots[...] = lax.broadcasted_iota(jnp.int32, spots.shape, 0).astype(F32).astype(BF)
     spread[...] = jnp.where(
         lax.broadcasted_iota(jnp.int32, spread.shape, 0)
@@ -247,23 +247,32 @@
         rel_t[:, at] = (rel_rows * 0.5).astype(BF)
         return 0
 
+    def row_slot(dz, at, n):
+        return rows.at[dz, pl.ds(pl.multiple_of(core * CHUNK + at, n), n)]
+
+    ag = gather(row_slot, ag_s, ag_r)
+
+    def pass_on(p):
+        at = pl.ds(pl.multiple_of(core * CHUNK + p * PIECE, PIECE), PIECE)
+        rows[0, at] = held[0, p * PIECE : (p + 1) * PIECE, :]
+        gather_piece(ag, p)
+
     lax.fori_loop(0, n_chunk, tables, 0, unroll=8)
     lax.fori_loop(0, n_block // 2, count_block, 0, unroll=4)
+    if comm:
+        pl.semaphore_wait(barrier, len(peers))
+    exchange_start(0)
+    lax.fori_loop(n_block // 2, n_block, count_block, 0, unroll=4)
+    lax.fori_loop(0, n_block // 4, query_block, 0, unroll=2)
     end_round(0, 0)
-    lax.fori_loop(n_block // 2, n_block, count_block, 0, unroll=4)
+    lax.fori_loop(n_block // 4, n_block // 2, query_block, 0, unroll=2)
     end_round(0, 1)
-    lax.fori_loop(0, n_block // 4, query_block, 0, unroll=2)
-    end_round(0, 2)
-    rows[0, span(core, CHUNK)] = held[0]
-
-    def row_slot(dz, at, n):
-        return rows.at[dz, pl.ds(pl.multiple_of(core * CHUNK + at, n), n)]
-
-    ag = gather(row_slot, ag_s, ag_r)
-    gather_start(ag)
-    lax.fori_loop(n_block // 4, 3 * n_block // 4, query_block, 0, unroll=2)
+    scale_col[...] = jnp.broadcast_to(scale_row(r), (128, CHUNK)).T
+    accum_col[...] = jnp.broadcast_to(accum[:, span(r, CHUNK)], (128, CHUNK)).T
+    lax.fori_loop(n_block // 2, 3 * n_block // 4, query_block, 0, unroll=2)
+    end_round(0, 2, pass_on)
+    lax.fori_loop(3 * n_block // 4, n_block, query_block, 0, unroll=2)
     gather_forward(ag)
-    lax.fori_loop(3 * n_block // 4, n_block, query_block, 0, unroll=2)
 
     def score_pair(dz):
         a = pair_of(dz)
@@ -354,19 +363,19 @@
     dg = Reduce(dg_own, dg_mate_in, dg_far_in, dg_mate_out, dg_far_out, dm_s, dm_r, df_s, df_r)
     sg = Reduce(sg_own, sg_mate_in, sg_far_in, sg_mate_out, sg_far_out, sm_s, sm_r, sf_s, sf_r)
 
-    got(ag["m0"])
+    got(*[ag["mate", p] for p in range(PIECES)])
     score_pair(0)
     dg.give(0)
     gather_mate(ag)
-    got(ag["m1"])
+    got(ag["relay", 1])
     score_pair(1)
     dg.give(1)
     gather_last(ag)
-    got(ag["m2"])
+    got(ag["relay", 2])
     score_pair(2)
     dg.give(2)
     dg.send(1)
-    got(ag["m3"])
+    got(ag["relay", 3])
     score_pair(3)
     dg.give(3)
     dg.send(2)
@@ -388,32 +397,42 @@
     sg.give(1)
     sg.send(2)
     held[1] = (dg.total() * 0.5).astype(BF)
-    start_round(1, 0)
+    exchange_start(1)
     source_pair(3)
     sg.give(3)
     sg.send(1)
     source_pair(0)
     sg.give(0)
     sg.send(3)
-    for j in range(3):
-        end_round(1, j)
-
-    grad_t = (sg.total() + held[1].astype(F32)).T
-    state = accum[:, span(r, CHUNK)] + jnp.mean(grad_t * grad_t, axis=0, keepdims=True)
-    out_accum[...] = state
-    values_t = turned(share[...]) * scale_row(r)
-    updated = values_t - LEARN_RATE * grad_t / (jnp.sqrt(state) + ROOT_EPSILON)
-    out_codes[span(r, CHUNK), :] = (updated / scale_row(r)).T.astype(BF)
-
     def out_slot(dz, at, n):
         return out_codes.at[pl.ds(pl.multiple_of((pair_of(dz) * 2 + core) * CHUNK + at, n), n)]
 
     og = gather(out_slot, o_s, o_r, True)
-    gather_start(og)
+
+    def wide(block):
+        return jnp.concatenate([block, block], axis=1)
+
+    def update(p):
+        at = slice(p * PIECE, (p + 1) * PIECE)
+        here = pl.ds(pl.multiple_of(r * CHUNK + p * PIECE, PIECE), PIECE)
+        grad = acc[at, :] + held[1, at, :].astype(F32)
+        state = accum_col[at, :] + jnp.mean(grad * grad, axis=1, keepdims=True)
+        state_col[at, :] = state
+        scale = wide(scale_col[at, :])
+        values = codes[here, :].astype(F32) * scale
+        updated = values - LEARN_RATE * grad / wide(jnp.sqrt(state) + ROOT_EPSILON)
+        out_codes[here, :] = (updated / scale).astype(BF)
+        gather_piece(og, p)
+
+    end_round(1, 0)
+    end_round(1, 1)
+    acc[0:CHUNK, :] = sg.total()
+    end_round(1, 2, update)
     gather_forward(og)
     gather_mate(og)
+    out_accum[...] = state_col[...].T[0:1, :]
     gather_last(og)
-    got(og["m0"], og["m1"], og["m3"], og["m2"])
+    got(*[og["mate", p] for p in range(PIECES)], *[og["relay", dz] for dz in (1, 3, 2)])
     left(*og.values(), *ag.values())
     dg.done()
     sg.done()
@@ -433,6 +452,9 @@
         pltpu.VMEM(one, BF),
         pltpu.VMEM((n, width), BF),
         pltpu.VMEM((1, n), BF),
+        pltpu.VMEM((CHUNK, 128), F32),
+        pltpu.VMEM((CHUNK, 128), F32),
+        pltpu.VMEM((CHUNK, 128), F32),
         pltpu.VMEM((1, n), F32),
         pltpu.VMEM(relations.shape, BF),
         pltpu.VMEM(edges.shape, jnp.int32),
@@ -458,9 +480,9 @@
     ]
     for _ in range(2):
         scratch += [pltpu.VMEM((4,) + one, BF), pltpu.VMEM((3,) + one, BF)] * 2
-    scratch += [sem((7,)), sem((2, 3, 3, 3)), sem((2, 3, 3, 3)), sem((10,)), sem((10,))]
+    scratch += [sem((7,)), sem((2, 3, PIECES, 3)), sem((2, 3, PIECES, 3)), sem((19,)), sem((19,))]
     scratch += [sem((4,)), sem((4,)), sem((3,)), sem((3,))] * 2
-    scratch += [sem((10,)), sem((10,))]
+    scratch += [sem((19,)), sem((19,))]
     return pl.pallas_call(
         functools.partial(kernel, comm),
         out_shape=(
@@ -473,7 +495,7 @@
         compiler_params=pltpu.CompilerParams(
             collective_id=0 if comm else None,
             has_side_effects=True,
-            vmem_limit_bytes=50 << 20,
+            vmem_limit_bytes=58 << 20,
         ),
     )(
         matching, counts, codes, scales.reshape(1, n), accum.reshape(1, n), relations, edges,

time: 99.4 us -> 92.6 us (0.932)
  Pallas kernels: 91.9 us -> 87 us
  local copies, waits for them, and re-layouts: 5.13 us -> 3.44 us
    pallas_call x1, Pallas kernels: 91.9 us -> 87 us  [call(): pl.pallas_call(functools.partial(kernel, comm), out_shape=(jax.ShapeDtype...]
    unnamed x14 -> x6, local copies, waits for them, and re-layouts: 5.12 us -> 2.83 us
where the time goes in v3:
time: 92.6 us; the launch traced here: 92.4 us
  Pallas kernels  87 us (94%)
  local copies, waits for them, and re-layouts  3.44 us (4%)
  between operations  1.97 us (2%)
    pallas_call x1, Pallas kernels, call(): pl.pallas_call(functools.partial(kernel, comm), out_shape=(jax.ShapeDtype...  87 us
    unnamed x6, local copies, waits for them, and re-layouts  2.83 us

profile of v3, /device:TPU:1, one launch (start us, length us, event | category | flops | bytes accessed | tf_op | source)
XLA Modules:
  0.0 92.4 jit_solution(7635546833831746522)
XLA Ops:
  0.6 0.0 copy-start
  1.9 0.0 copy-done
  2.0 0.6 reshape.13.scales_hbm
  2.6 87.0 %shard_map.95 = (bf16[2048,256]{1,0:T(8,128)(2,1)}, f32[1,256]{1,0:T(1,128)}) custom-call(s32[1]{0:T(128)S(6)} %copy.12.matching, s32[1]{0:T(128)S(6)} %copy.13.counts, bf16[2048,256]{1,0:T(8,128)(2,1)} %codes_hbm.1, bf16[1,2048]{1,0:T(2,128)(2,1)} %reshape.13.scales_hbm, f32[1,2048]{1,0:T(1,128)} %bitcast.2, bf16[64,256]{1,0:T(8,128)(2,1)} %relations_hbm.1, ...), custom_call_target="tpu_custom_call" | custom-call | tf_op jit(solution)/shard_map/pallas_call | solution.py:486
  89.6 0.0 copy-start.1
  89.6 2.3 %copy.14 = bf16[2048,256]{1,0:T(8,128)(2,1)} copy(bf16[2048,256]{1,0:T(8,128)(2,1)} %get-tuple-element.8) | data formatting | bytes 2097152
  91.9 0.0 copy-done.1
  91.9 0.6 copy.15
Async XLA Ops:
  0.6 1.3 %copy-start = (bf16[2048]{0:T(1024)(128)(2,1)S(1)}, bf16[2048]{0:T(1024)(128)(2,1)}, u32[]{:S(2)}) copy-start(bf16[2048]{0:T(1024)(128)(2,1)} %param.9) | copy-start | bytes 12292
  89.6 2.3 %copy-start.1 = (f32[1,256]{1,0:T(1,128)S(1)}, f32[1,256]{1,0:T(1,128)}, u32[]{:S(2)}) copy-start(f32[1,256]{1,0:T(1,128)} %get-tuple-element.5) | copy-start | bytes 3076

commit v4 on v3

--- a/solution.py
+++ b/solution.py
@@ -396,14 +396,14 @@
     source_pair(1)
     sg.give(1)
     sg.send(2)
-    held[1] = (dg.total() * 0.5).astype(BF)
-    exchange_start(1)
     source_pair(3)
     sg.give(3)
     sg.send(1)
     source_pair(0)
     sg.give(0)
     sg.send(3)
+    held[1] = (dg.total() * 0.5).astype(BF)
+    exchange_start(1)
     def out_slot(dz, at, n):
         return out_codes.at[pl.ds(pl.multiple_of((pair_of(dz) * 2 + core) * CHUNK + at, n), n)]
 

time: 92.6 us -> 91.7 us (level)
  no operation moved by 1% of the time
where the time goes in v4:
time: 91.7 us; the launch traced here: 91.6 us
  Pallas kernels  86.2 us (94%)
  local copies, waits for them, and re-layouts  3.44 us (4%)
  between operations  1.97 us (2%)
    pallas_call x1, Pallas kernels, call(): pl.pallas_call(functools.partial(kernel, comm), out_shape=(jax.ShapeDtype...  86.2 us
    unnamed x6, local copies, waits for them, and re-layouts  2.83 us

profile of v4, /device:TPU:1, one launch (start us, length us, event | category | flops | bytes accessed | tf_op | source)
XLA Modules:
  0.0 91.6 jit_solution(17245806485739882769)
XLA Ops:
  0.6 0.0 copy-start
  1.9 0.0 copy-done
  2.0 0.6 reshape.13.scales_hbm
  2.6 86.2 %shard_map.95 = (bf16[2048,256]{1,0:T(8,128)(2,1)}, f32[1,256]{1,0:T(1,128)}) custom-call(s32[1]{0:T(128)S(6)} %copy.12.matching, s32[1]{0:T(128)S(6)} %copy.13.counts, bf16[2048,256]{1,0:T(8,128)(2,1)} %codes_hbm.1, bf16[1,2048]{1,0:T(2,128)(2,1)} %reshape.13.scales_hbm, f32[1,2048]{1,0:T(1,128)} %bitcast.2, bf16[64,256]{1,0:T(8,128)(2,1)} %relations_hbm.1, ...), custom_call_target="tpu_custom_call" | custom-call | tf_op jit(solution)/shard_map/pallas_call | solution.py:486
  88.7 0.0 copy-start.1
  88.7 2.3 %copy.14 = bf16[2048,256]{1,0:T(8,128)(2,1)} copy(bf16[2048,256]{1,0:T(8,128)(2,1)} %get-tuple-element.8) | data formatting | bytes 2097152
  91.0 0.0 copy-done.1
  91.0 0.6 copy.15
Async XLA Ops:
  0.6 1.3 %copy-start = (bf16[2048]{0:T(1024)(128)(2,1)S(1)}, bf16[2048]{0:T(1024)(128)(2,1)}, u32[]{:S(2)}) copy-start(bf16[2048]{0:T(1024)(128)(2,1)} %param.9) | copy-start | bytes 12292
  88.7 2.3 %copy-start.1 = (f32[1,256]{1,0:T(1,128)S(1)}, f32[1,256]{1,0:T(1,128)}, u32[]{:S(2)}) copy-start(f32[1,256]{1,0:T(1,128)} %get-tuple-element.5) | copy-start | bytes 3076
